TPU v7x, 32 devices: a whole 2x2x4 slice. The times are simulated.
32 devices in a mesh: tok: 8 (over z, x), head: 4 (over y, core).
Axes of the slice: x: 2, y: 2, z: 4, core: 2. Of those that a mesh axis runs over, the one named last changes fastest.
Arguments:
- queries: bfloat16 [128, 8192], P('tok', 'head'), may hold values from -40 to 40
- keys: bfloat16 [8192, 1024], P('tok', 'head'), may hold values from -13 to 13
- values: bfloat16 [8192, 1024], P('tok', 'head'), may hold values from -6 to 6
- out_grad: bfloat16 [128, 8192], P('head', 'tok'), may hold values from -6 to 6
- out_weight: bfloat16 [8192, 8192], P('head', 'tok'), may hold values from -0.0625 to 0.0625
- frame_end: int32 [128], replicated, may hold values from 1 to 64
Outputs:
- query_grad: float32 [128, 8192], P('tok', 'head')
- key_gradient: float32 [8192, 1024], P('tok', 'head')
- value_gradient: float32 [8192, 1024], P('tok', 'head')
- out_weight_grad: float32 [8192, 8192], P('head', 'tok')
All inputs are finite; a program needn't handle non-finite values.
Results may differ from a plain program's by a relative error of at most 0.014.
Values may be sent and summed in bfloat16 or wider, within the bound.
A program may use at most 64 MiB of HBM per device.

v0:
```python
import math

import jax
import jax.numpy as jnp
from jax import lax
from jax.sharding import PartitionSpec as P

QUERY_HEADS = 64
KEY_VALUE_HEADS = 8
HEAD_SIZE = 128
FRAME = 128


NEGATIVE = -1e30


def combined_all(value, axis, join):
    pieces = jax.tree.map(lambda part: lax.all_gather(part, axis), value)
    head = jax.tree.map(lambda part: part[0], pieces)
    tail = jax.tree.map(lambda part: part[1:], pieces)
    subtotal, _ = lax.scan(lambda subtotal, piece: (join(subtotal, piece), None), head, tail)
    return subtotal


def merge_totals(first, second):
    first_peak, first_total = first
    second_peak, second_total = second
    joined = jnp.maximum(first_peak, second_peak)
    summed = first_total * jnp.exp(first_peak - joined) + second_total * jnp.exp(
        second_peak - joined
    )
    return (joined, summed)


def contract(left, right, left_dim, right_dim):
    return lax.dot_general(
        left, right, (((left_dim,), (right_dim,)), ((), ())), preferred_element_type=jnp.float32
    )


def body(queries, keys, values, out_grad, out_weight, frame_end):
    score_scale = 1.0 / math.sqrt(HEAD_SIZE)
    heads_per_group = QUERY_HEADS // KEY_VALUE_HEADS
    row_count = frame_end.shape[0]
    key_count = keys.shape[0]
    local_groups = keys.shape[1] // HEAD_SIZE
    local_heads = local_groups * heads_per_group
    full_grad = lax.all_gather(out_grad, "head", axis=0, tiled=True)
    grad_terms = contract(full_grad, out_weight, 1, 1)
    all_queries = lax.all_gather(queries, "tok", axis=0, tiled=True)
    positions = lax.axis_index("tok") * key_count + jnp.arange(key_count, dtype=jnp.int32)
    visible = (positions // FRAME)[None, :] < frame_end[:, None]
    query_heads = all_queries.reshape(row_count, local_heads, HEAD_SIZE)
    key_head_rows = keys.reshape(key_count, local_groups, HEAD_SIZE)
    value_head_rows = values.reshape(key_count, local_groups, HEAD_SIZE)
    head_index = jnp.arange(local_heads, dtype=jnp.int32)

    def head_scores(member):
        query_block = lax.dynamic_index_in_dim(query_heads, member, 1, False)
        key_block = lax.dynamic_index_in_dim(key_head_rows, member // heads_per_group, 1, False)
        return contract(query_block, key_block, 1, 1) * score_scale

    def local_totals(member):
        masked = jnp.where(visible, head_scores(member), NEGATIVE)
        row_peak = jnp.max(masked, axis=1)
        row_total = jnp.sum(jnp.where(visible, jnp.exp(masked - row_peak[:, None]), 0.0), axis=1)
        return (row_peak, row_total)

    row_peaks, row_totals = lax.map(local_totals, head_index)
    row_peaks, row_totals = combined_all((row_peaks, row_totals), "tok", merge_totals)

    def probabilities(member, scores):
        row_peak = lax.dynamic_index_in_dim(row_peaks, member, 0, False)
        row_total = lax.dynamic_index_in_dim(row_totals, member, 0, False)
        return jnp.where(visible, jnp.exp(scores - row_peak[:, None]) / row_total[:, None], 0.0)

    def output_part(member):
        value_block = lax.dynamic_index_in_dim(value_head_rows, member // heads_per_group, 1, False)
        prob_low = probabilities(member, head_scores(member)).astype(jnp.bfloat16)
        return jnp.dot(prob_low, value_block, preferred_element_type=jnp.float32)

    output_parts = lax.map(output_part, head_index)
    output_terms = jnp.transpose(output_parts, (1, 0, 2)).reshape(
        row_count, local_heads * HEAD_SIZE
    )
    grad_share = lax.psum_scatter(grad_terms, "tok", scatter_dimension=0, tiled=True).astype(
        jnp.bfloat16
    )
    output_share = lax.psum_scatter(output_terms, "tok", scatter_dimension=0, tiled=True).astype(
        jnp.bfloat16
    )
    attn_out, head_grad = (
        lax.all_gather(output_share, "tok", axis=0, tiled=True),
        lax.all_gather(grad_share, "tok", axis=0, tiled=True),
    )
    out_weight_grad = contract(attn_out, full_grad, 0, 0)
    grad_heads = head_grad.reshape(row_count, local_heads, HEAD_SIZE)
    products = head_grad.astype(jnp.float32) * attn_out.astype(jnp.float32)
    deltas = jnp.sum(products.reshape(row_count, local_heads, HEAD_SIZE), axis=2)
    key_parts = []
    value_parts = []
    query_groups = []
    for kv_group in range(local_groups):
        key_block = key_head_rows[:, kv_group, :]
        value_block = value_head_rows[:, kv_group, :]

        def backward_head(running, member):
            key_total, value_total = running
            head_number = kv_group * heads_per_group + member
            query_block = lax.dynamic_index_in_dim(query_heads, head_number, 1, False)
            grad_block = lax.dynamic_index_in_dim(grad_heads, head_number, 1, False)
            scores = contract(query_block, key_block, 1, 1) * score_scale
            prob_values = probabilities(head_number, scores)
            prob_low = prob_values.astype(jnp.bfloat16)
            delta_column = lax.dynamic_index_in_dim(deltas, head_number, 1, True)
            prob_grad = contract(grad_block, value_block, 1, 1)
            score_grad = (prob_values * (prob_grad - delta_column)).astype(jnp.bfloat16)
            value_total = value_total + contract(prob_low, grad_block, 0, 0)
            key_total = key_total + contract(score_grad, query_block, 0, 0) * score_scale
            query_part = (
                jnp.dot(score_grad, key_block, preferred_element_type=jnp.float32) * score_scale
            )
            return ((key_total, value_total), query_part)

        empty_rows = jnp.zeros((key_count, HEAD_SIZE), jnp.float32)
        (key_total, value_total), query_part = lax.scan(
            backward_head, (empty_rows, empty_rows), jnp.arange(heads_per_group, dtype=jnp.int32)
        )
        key_parts.append(key_total)
        value_parts.append(value_total)
        query_groups.append(query_part)
    key_gradient = jnp.concatenate(key_parts, axis=1)
    value_gradient = jnp.concatenate(value_parts, axis=1)
    query_stack = jnp.concatenate(query_groups, axis=0)
    query_terms = jnp.transpose(query_stack, (1, 0, 2)).reshape(row_count, local_heads * HEAD_SIZE)
    query_grad = lax.psum_scatter(
        query_terms.astype(jnp.bfloat16), "tok", scatter_dimension=0, tiled=True
    ).astype(jnp.float32)
    return (query_grad, key_gradient, value_gradient, out_weight_grad)


def solution(mesh):
    placed = (
        P("tok", "head"),
        P("tok", "head"),
        P("tok", "head"),
        P("head", "tok"),
        P("head", "tok"),
        P(),
    )
    return jax.shard_map(
        body,
        mesh=mesh,
        in_specs=placed,
        out_specs=(P("tok", "head"), P("tok", "head"), P("tok", "head"), P("head", "tok")),
        check_vma=False,
    )
```

profile of v0, /device:TPU:0, one launch (start us, length us, event | category | flops | bytes accessed | tf_op | source)
XLA Modules:
  0.0 555.3 jit_solution(10038164903424182582)
XLA Ops:
  7.2 7.4 %all_gather.29 = bf16[128,1024]{1,0:T(8,128)(2,1)S(1)} all-gather(bf16[32,1024]{1,0:T(8,128)(2,1)} %param.19), channel_id=1, replica_groups=mesh['tok'=8,'head'=4] {'head'}, dimensions={0}, use_global_device_ids=true | all-gather | bytes 327680 | tf_op jit(solution)/shard_map/all_gather | solution.py:48
  14.7 4.7 fusion.102
  19.5 32.6 %all_gather.24 = bf16[128,2048]{1,0:T(8,128)(2,1)S(1)} all-gather(bf16[16,2048]{1,0:T(8,128)(2,1)S(1)} %copy-done.7), channel_id=1, replica_groups=mesh['tok'=8,'head'=4] {'tok'}, dimensions={0}, use_global_device_ids=true | all-gather | bytes 589824 | tf_op jit(solution)/shard_map/all_gather | solution.py:50
  53.2 74.5 %while.73 = (s32[]{:T(128)}, f32[16,128]{1,0:T(8,128)S(1)}, f32[16,128]{1,0:T(8,128)S(1)}, s32[16]{0:T(128)S(1)}, bf16[128,16,128]{2,0,1:T(8,128)(2,1)S(1)}, /*i...) while((s32[]{:T(128)}, f32[16,128]{1,0:T(8,128)S(1)}, ...), condition=%wide.region_4.5_spmd.clone, body=%wide.region_1.4_spmd.clone.sunk | while | flops 34602772 | bytes 1356674 | solution.py:69
  127.7 30.5 %all-gather.1 = f32[128,128]{1,0:T(8,128)S(1)} all-gather(f32[16,128]{1,0:T(8,128)S(1)} %get-tuple-element.470), channel_id=3, replica_groups=mesh['tok'=8,'head'=4] {'tok'}, dimensions={0}, use_global_device_ids=true | all-gather | bytes 73728 | tf_op jit(solution)/shard_map/all_gather | solution.py:18
  158.2 30.5 %all-gather = f32[128,128]{1,0:T(8,128)S(1)} all-gather(f32[16,128]{1,0:T(8,128)S(1)} %get-tuple-element.469), channel_id=2, replica_groups=mesh['tok'=8,'head'=4] {'tok'}, dimensions={0}, use_global_device_ids=true | all-gather | bytes 73728 | tf_op jit(solution)/shard_map/all_gather | solution.py:18
  189.0 1.2 copy.50
  190.2 79.1 %while.74 = (s32[]{:T(128)}, f32[16,128,128]{2,1,0:T(8,128)S(1)}, s32[16]{0:T(128)S(1)}, bf16[128,16,128]{2,0,1:T(8,128)(2,1)S(1)}, bf16[1024,2,128]{2,0,1:T(8,1...) while((s32[]{:T(128)}, f32[16,128,128]{2,1,0:T(8,128)S(1)}, ...), condition=%wide.region_8.9_spmd.clone, body=%wide.region_7.8_spmd.clone.sunk | while | flops 67895320 | bytes 632710 | solution.py:82
  269.3 1.2 copy_bitcast_fusion
  271.0 1.8 slice_bitcast_fusion.2
  273.0 1.1 copy.63
  275.1 31.8 %all_gather.30 = bf16[128,2048]{1,0:T(8,128)(2,1)S(1)} all-gather(bf16[16,2048]{1,0:T(8,128)(2,1)S(1)} %convert_element_type.46), channel_id=1, replica_groups=mesh['tok'=8,'head'=4] {'tok'}, dimensions={0}, use_global_device_ids=true | all-gather | bytes 589824 | tf_op jit(solution)/shard_map/all_gather | solution.py:94
  308.6 26.6 %reduce-scatter.6.cloned.1.call-done = f32[16,2048]{1,0:T(8,128)} async-done(((f32[128,2048]{1,0:T(8,128)}), f32[16,2048]{1,0:T(8,128)}) %reduce-scatter.6.cloned.1.call-update) | async-done | bytes 131088 | tf_op jit(solution)/shard_map/reduce_scatter | solution.py:89
  336.0 31.5 %all_gather.31 = bf16[128,2048]{1,0:T(8,128)(2,1)S(1)} all-gather(bf16[16,2048]{1,0:T(8,128)(2,1)S(1)} %convert_element_type.48), channel_id=1, replica_groups=mesh['tok'=8,'head'=4] {'tok'}, dimensions={0}, use_global_device_ids=true | all-gather | bytes 589824 | tf_op jit(solution)/shard_map/all_gather | solution.py:93
  368.4 1.2 multiply_bitcast_fusion
  369.5 1.2 copy.70
  370.7 1.6 reduce_sum.21
  373.1 56.0 %while.76 = (s32[]{:T(128)}, f32[1024,128]{1,0:T(8,128)S(1)}, f32[1024,128]{1,0:T(8,128)S(1)}, bf16[8,128,128]{2,1,0:T(8,128)(2,1)}, s32[8]{0:T(128)S(1)}, /*ind...) while((s32[]{:T(128)}, f32[1024,128]{1,0:T(8,128)S(1)}, ...), condition=%wide.region_14.15_spmd.clone, body=%wide.region_13.14_spmd.clone.sunk | while | flops 169623552 | bytes 5448974 | solution.py:126
  377.1 1.1 convolution_add_fusion.5
  379.0 1.1 fusion.198
  384.1 1.1 convolution_add_fusion.5
  391.1 1.1 convolution_add_fusion.5
  398.1 1.1 convolution_add_fusion.5
  405.0 1.1 convolution_add_fusion.5
  412.0 1.1 convolution_add_fusion.5
  419.0 1.1 convolution_add_fusion.5
  426.0 1.1 convolution_add_fusion.5
  429.1 56.3 %while.75 = (s32[]{:T(128)}, f32[1024,128]{1,0:T(8,128)S(1)}, f32[1024,128]{1,0:T(8,128)S(1)}, bf16[8,128,128]{2,1,0:T(8,128)(2,1)S(1)}, s32[8]{0:T(128)S(1)}, /...) while((s32[]{:T(128)}, f32[1024,128]{1,0:T(8,128)S(1)}, ...), condition=%wide.region_12.13_spmd.clone, body=%wide.region_11.12_spmd.clone.sunk | while | flops 169623552 | bytes 5448954 | solution.py:126
  433.8 1.1 convolution_add_fusion.4
  435.1 1.1 fusion.182
  440.8 1.1 convolution_add_fusion.4
  442.1 1.1 fusion.182
  447.8 1.1 convolution_add_fusion.4
  449.2 1.1 fusion.182
  454.9 1.1 convolution_add_fusion.4
  456.2 1.1 fusion.182
  461.9 1.1 convolution_add_fusion.4
  463.2 1.1 fusion.182
  469.0 1.1 convolution_add_fusion.4
  470.3 1.1 fusion.182
  476.0 1.1 convolution_add_fusion.4
  477.3 1.1 fusion.182
  483.0 1.1 convolution_add_fusion.4
  484.4 1.1 fusion.182
  486.4 1.5 pad_maximum_fusion
  487.8 4.7 fusion.103
  492.5 54.8 %reduce-scatter.8.cloned.1.call-done = bf16[16,2048]{1,0:T(8,128)(2,1)} async-done(((bf16[128,2048]{1,0:T(8,128)(2,1)}), bf16[16,2048]{1,0:T(8,128)(2,1)}) %reduce-scatter.8.cloned.1.call-update) | async-done | bytes 65552 | tf_op jit(solution)/shard_map/reduce_scatter | solution.py:136
  547.3 1.5 convert_element_type.52
  (295 shorter events, 103.0 us)
Async XLA Ops:
  7.2 12.3 %copy-start.7 = (bf16[16,2048]{1,0:T(8,128)(2,1)S(1)}, bf16[16,2048]{1,0:T(8,128)(2,1)}, u32[]{:S(2)}) copy-start(bf16[16,2048]{1,0:T(8,128)(2,1)} %param.16) | copy-start | bytes 196612
  7.2 267.0 %reduce-scatter.4.cloned.1.call-start = ((), (), s32[]{:S(2)}) async-start(), calls=%async_computation.3 | async-start | bytes 1179648 | tf_op jit(solution)/shard_map/reduce_scatter | solution.py:86
  14.7 38.0 %copy-start.6 = (bf16[1024,256]{1,0:T(8,128)(2,1)S(1)}, bf16[1024,256]{1,0:T(8,128)(2,1)}, u32[]{:S(2)}) copy-start(bf16[1024,256]{1,0:T(8,128)(2,1)} %param.17) | copy-start | bytes 1572868
  19.4 33.8 %copy-start.8 = (s32[128]{0:T(128)S(1)}, s32[128]{0:T(128)}, u32[]{:S(2)}) copy-start(s32[128]{0:T(128)} %param.21) | copy-start | bytes 1540
  19.4 315.7 %reduce-scatter.6.cloned.1.call-start = ((), (), s32[]{:S(2)}) async-start(), calls=%async_computation.4 | async-start | bytes 1179648 | tf_op jit(solution)/shard_map/reduce_scatter | solution.py:89
  269.3 1.3 copy-start.3
  269.3 1.3 copy-start.4
  270.5 276.7 %reduce-scatter.8.cloned.1.call-start = ((), (), s32[]{:S(2)}) async-start(), calls=%async_computation.5 | async-start | bytes 589824 | tf_op jit(solution)/shard_map/reduce_scatter | solution.py:136
  306.8 0.8 copy-start.2
  367.6 0.8 copy-start
  429.1 56.4 %copy-start.5 = (bf16[8,128,128]{2,1,0:T(8,128)(2,1)S(1)}, bf16[8,128,128]{2,1,0:T(8,128)(2,1)}, u32[]{:S(2)}) copy-start(bf16[8,128,128]{2,1,0:T(8,128)(2,1)} %get-tuple-element.475) | copy-start | bytes 786436
  485.4 2.4 copy-start.1
Sparse Core Ops, SparseCore 0:
  19.5 65.0 reduce-scatter.3
  270.7 64.4 reduce-scatter.5
  486.5 60.7 reduce-scatter.7
where the time goes:
time: 562 us; the launch traced here: 555 us
  blocking collectives  164 us (29%)
  loops' own time  145 us (26%)
  matrix products  96.6 us (17%)
  waiting for transfers between devices  81.4 us (14%)
  local copies, waits for them, and re-layouts  41.5 us (7%)
  between operations  14.1 us (3%)
  other arithmetic  12.8 us (2%)
    dot_general x82, matrix products, contract(): lax.dot_general(left, right, (((left_dim,), (right_dim,)), ((), ())), pre...  81.3 us
    another operation x1, loops' own time, body(): output_parts = lax.map(output_part, head_index)  62.9 us
    all_gather x2, blocking collectives, combined_all(): pieces = jax.tree.map(lambda part: lax.all_gather(part, axis), value)  61 us
    reduce_scatter x1, waiting for transfers between devices, body(): lax.psum_scatter(query_terms.astype(jnp.bfloat16), 'tok', scatter_dimensi...  54.8 us
    another operation x1, loops' own time, body(): row_peaks, row_totals = lax.map(local_totals, head_index)  54.5 us
    all_gather x1, blocking collectives, body(): all_queries = lax.all_gather(queries, 'tok', axis=0, tiled=True)  32.6 us
    all_gather x1, blocking collectives, body(): lax.all_gather(grad_share, 'tok', axis=0, tiled=True)  31.8 us
    all_gather x1, blocking collectives, body(): lax.all_gather(output_share, 'tok', axis=0, tiled=True)  31.5 us
  transfers between devices with their start and end apart: 3, of which 2 were waited for; matrix products, arithmetic and copies ran while one was open for 9% of the time, Pallas kernels for 0%

commit v1 on v0

v1 whole, which is shorter than its diff:
```python
import functools
import math

import jax
import jax.numpy as jnp
from jax import lax
from jax.experimental import pallas as pl
from jax.experimental.pallas import tpu as pltpu
from jax.sharding import PartitionSpec as P

QUERY_HEADS = 64
KEY_VALUE_HEADS = 8
HEAD_SIZE = 128
FRAME = 128
HEADS_PER_GROUP = QUERY_HEADS // KEY_VALUE_HEADS

MASKED = -1e30
LOWEST = -1e29
SCALE = 1.0 / math.sqrt(HEAD_SIZE)
LOG2E = math.log2(math.e)
BF16 = jnp.bfloat16
F32 = jnp.float32
MESH = pl.DeviceIdType.MESH


def dot(left, right, left_dim=1, right_dim=0):
    return lax.dot_general(
        left, right, (((left_dim,), (right_dim,)), ((), ())), preferred_element_type=F32
    )


def send(src, dst, send_sem, recv_sem, peer):
    return pltpu.make_async_remote_copy(
        src_ref=src,
        dst_ref=dst,
        send_sem=send_sem,
        recv_sem=recv_sem,
        device_id=peer,
        device_id_type=MESH,
    )


def kernel(
    tok, head, q_ref, k_hbm, v_hbm, og_ref, ow_hbm, fe_ref,
    dq_ref, dk_ref, dv_ref, att_ref, fg_ref,
    k_ref, v_ref, ow_ref, kt_ref, vt_ref, fg, qall, gsend, grecv, hgall, pbuf, mbuf,
    osend, orecv, ssend, srecv, tall, atall, dqsend, dqrecv,
    load_sem, og_s, og_r, q_s, q_f, q_r, g_s, g_r, h_s, h_f, h_r, o_s, o_r, s_s, s_r,
    t_s, t_f, t_r, a_s, a_f, a_r, dq_s, dq_r,
):
    me = lax.axis_index("tok")
    me_head = lax.axis_index("head")
    pairs = tok // 2
    my_pair = me // 2
    side = me % 2
    partner = me + 1 - 2 * side
    rows, width = q_ref.shape
    key_count = k_ref.shape[0]
    groups = k_ref.shape[1] // HEAD_SIZE
    lanes = HEADS_PER_GROUP * rows

    loads = [
        pltpu.make_async_copy(src, dst, load_sem.at[i])
        for i, (src, dst) in enumerate(((ow_hbm, ow_ref), (k_hbm, k_ref), (v_hbm, v_ref)))
    ]
    for load in loads:
        load.start()
    qall[me] = q_ref[...]
    fg[me_head] = og_ref[...]

    def tok_peer(d):
        return lax.rem(me + d, tok)

    def head_peer(d):
        return lax.rem(me_head + d, head)

    barrier = pltpu.get_barrier_semaphore()

    @pl.loop(1, tok)
    def _(d):
        pl.semaphore_signal(barrier, inc=1, device_id={"tok": tok_peer(d)}, device_id_type=MESH)

    @pl.loop(1, head)
    def _(d):
        pl.semaphore_signal(barrier, inc=1, device_id={"head": head_peer(d)}, device_id_type=MESH)

    pl.semaphore_wait(barrier, tok + head - 2)

    def og_copy(owner, peer):
        return send(fg.at[owner], fg.at[owner], og_s.at[peer], og_r.at[owner], {"head": peer})

    @pl.loop(1, head)
    def _(d):
        og_copy(me_head, head_peer(d)).start()

    class Gather:
        def __init__(self, buf, s, f, r):
            self.buf, self.s, self.f, self.r = buf, s, f, r

        def own(self, peer):
            return send(
                self.buf.at[me], self.buf.at[me], self.s.at[peer], self.r.at[me], {"tok": peer}
            )

        def relay(self, block):
            return send(
                self.buf.at[block], self.buf.at[block], self.f.at[block], self.r.at[block],
                {"tok": partner},
            )

        def arrived(self, block):
            return send(
                self.buf.at[block], self.buf.at[block], self.s.at[block], self.r.at[block],
                {"tok": partner},
            )

        def start(self):
            self.own(partner).start()

            @pl.loop(1, pairs)
            def _(d):
                self.own(2 * lax.rem(my_pair + d, pairs) + side).start()

        def forward(self, d):
            block = 2 * lax.rem(my_pair + d, pairs) + side
            self.arrived(block).wait_recv()
            self.relay(block).start()

        def wait_other(self, d):
            block = 2 * lax.rem(my_pair + d, pairs) + 1 - side
            self.arrived(block).wait_recv()

        def drain(self):
            self.own(partner).wait_send()

            @pl.loop(1, pairs)
            def _(d):
                block = 2 * lax.rem(my_pair + d, pairs) + side
                self.own(block).wait_send()
                self.relay(block).wait_send()

    class Scatter:
        def __init__(self, source, landing, s, r):
            self.source, self.landing, self.s, self.r = source, landing, s, r

        def to(self, peer):
            return send(
                self.source.at[peer], self.landing.at[me], self.s.at[peer], self.r.at[me],
                {"tok": peer},
            )

        def wait_all(self):
            @pl.loop(1, tok)
            def _(d):
                peer = tok_peer(d)
                send(
                    self.source.at[peer], self.landing.at[peer], self.s.at[peer],
                    self.r.at[peer], {"tok": peer},
                ).wait_recv()

        def drain(self):
            @pl.loop(1, tok)
            def _(d):
                self.to(tok_peer(d)).wait_send()

    query_gather = Gather(qall, q_s, q_f, q_r)
    grad_gather = Gather(hgall, h_s, h_f, h_r)
    stat_gather = Gather(tall, t_s, t_f, t_r)
    att_gather = Gather(atall, a_s, a_f, a_r)
    grad_scatter = Scatter(gsend, grecv, g_s, g_r)
    out_scatter = Scatter(osend, orecv, o_s, o_r)
    stat_scatter = Scatter(ssend, srecv, s_s, s_r)
    query_scatter = Scatter(dqsend, dqrecv, dq_s, dq_r)

    query_gather.start()

    for load in loads[1:]:
        load.wait()
    for g in range(groups):
        cols = slice(g * HEAD_SIZE, (g + 1) * HEAD_SIZE)
        kt_ref[g] = k_ref[:, cols].astype(F32).T.astype(BF16)
        vt_ref[g] = v_ref[:, cols].astype(F32).T.astype(BF16)

    loads[0].wait()

    @pl.loop(1, head)
    def _(d):
        peer = head_peer(d)
        send(fg.at[peer], fg.at[peer], og_s.at[peer], og_r.at[peer], {"head": peer}).wait_recv()

    full = fg[...].reshape(tok * rows, fg.shape[2])
    tile = min(256, width)

    @pl.loop(0, width // tile)
    def _(i):
        start = pl.multiple_of(i * tile, tile)
        part = dot(full, ow_ref[pl.ds(start, tile), :], 1, 1).astype(BF16)
        gsend[:, :, pl.ds(start, tile)] = part.reshape(tok, rows, tile)

    grecv[me] = gsend[me]

    @pl.loop(1, tok)
    def _(d):
        grad_scatter.to(tok_peer(d)).start()

    def stacked(buf, pair, g):
        pieces = []
        for one in range(2):
            block = buf[2 * pair + one]
            for h in range(HEADS_PER_GROUP):
                at = (g * HEADS_PER_GROUP + h) * HEAD_SIZE
                pieces.append(block[:, at : at + HEAD_SIZE])
        return jnp.concatenate(pieces, axis=0)

    token = lax.broadcasted_iota(jnp.int32, (key_count, 2 * lanes), 0)
    row8 = lax.broadcasted_iota(jnp.int32, (8, lanes), 0)

    def forward_pair(pair):
        limit = fe_ref[pair] * FRAME - me * key_count
        for g in range(groups):
            cols = slice(g * HEAD_SIZE, (g + 1) * HEAD_SIZE)
            scores = dot(k_ref[:, cols], stacked(qall, pair, g), 1, 1) * (SCALE * LOG2E)
            scores = jnp.where(token < limit, scores, MASKED)
            peak = jnp.maximum(jnp.max(scores, axis=0, keepdims=True), LOWEST)
            powers = jnp.exp2(scores - peak)
            total = jnp.sum(powers, axis=0, keepdims=True)
            low = powers.astype(BF16)
            pbuf[pair, g] = low
            mbuf[pair, g] = peak
            out = dot(vt_ref[g], low).astype(BF16)
            for one in range(2):
                part = slice(one * lanes, (one + 1) * lanes)
                osend[2 * pair + one, g] = out[:, part]
                ssend[2 * pair + one, g] = jnp.where(row8 == 0, peak[:, part], total[:, part])

    forward_pair_of = lambda d: lax.rem(my_pair + d, pairs)
    query_gather.arrived(partner).wait_recv()
    forward_pair(my_pair)
    orecv[me] = osend[me]
    srecv[me] = ssend[me]
    stat_scatter.to(partner).start()
    out_scatter.to(partner).start()
    if pairs > 1:
        query_gather.forward(1)

        @pl.loop(1, pairs)
        def _(d):
            @pl.when(d + 1 < pairs)
            def _():
                query_gather.forward(d + 1)

            query_gather.wait_other(d)
            pair = forward_pair_of(d)
            forward_pair(pair)
            for one in range(2):
                stat_scatter.to(2 * pair + one).start()
                out_scatter.to(2 * pair + one).start()

    grad_scatter.wait_all()
    hgall[me] = jnp.sum(grecv[...].astype(F32), axis=0).astype(BF16)
    grad_gather.start()

    stat_scatter.wait_all()
    out_scatter.wait_all()
    for g in range(groups):
        peaks = [srecv[j, g][0:1] for j in range(tok)]
        totals = [srecv[j, g][1:2] for j in range(tok)]
        peak = functools.reduce(jnp.maximum, peaks)
        weights = [jnp.exp2(one - peak) for one in peaks]
        inverse = 1.0 / functools.reduce(jnp.add, [a * b for a, b in zip(weights, totals)])
        merged = jnp.zeros((HEAD_SIZE, lanes), F32)
        for j in range(tok):
            merged += orecv[j, g].astype(F32) * weights[j]
        merged = (merged * inverse).astype(BF16).astype(F32)
        merged_rows = merged.T
        products = jnp.zeros((1, lanes), F32)
        grad_rows = []
        for h in range(HEADS_PER_GROUP):
            at = (g * HEADS_PER_GROUP + h) * HEAD_SIZE
            atall[me, :, at : at + HEAD_SIZE] = merged_rows[h * rows : (h + 1) * rows].astype(BF16)
            grad_rows.append(hgall[me, :, at : at + HEAD_SIZE].astype(F32))
        grad_t = jnp.concatenate(grad_rows, axis=0).T
        delta = jnp.sum(grad_t * merged, axis=0, keepdims=True)
        tall[me, g] = jnp.where(row8 == 0, peak, jnp.where(row8 == 1, inverse, delta))
    stat_gather.start()
    att_gather.start()

    dk_ref[...] = jnp.zeros_like(dk_ref)
    dv_ref[...] = jnp.zeros_like(dv_ref)

    def backward_pair(pair):
        for g in range(groups):
            cols = slice(g * HEAD_SIZE, (g + 1) * HEAD_SIZE)
            stats = jnp.concatenate([tall[2 * pair, g], tall[2 * pair + 1, g]], axis=1)
            factor = jnp.exp2(mbuf[pair, g] - stats[0:1]) * stats[1:2]
            grads = stacked(hgall, pair, g)
            probs = pbuf[pair, g].astype(F32) * factor
            prob_grad = dot(v_ref[:, cols], grads, 1, 1)
            score_grad = (probs * (prob_grad - stats[2:3])).astype(BF16)
            dv_ref[:, cols] += dot(probs.astype(BF16), grads)
            dk_ref[:, cols] += dot(score_grad, stacked(qall, pair, g)) * SCALE
            query_part = (dot(kt_ref[g], score_grad) * SCALE).astype(BF16)
            for one in range(2):
                dqsend[2 * pair + one, g] = query_part[:, one * lanes : (one + 1) * lanes]

    grad_gather.arrived(partner).wait_recv()
    stat_gather.arrived(partner).wait_recv()
    backward_pair(my_pair)
    dqrecv[me] = dqsend[me]
    query_scatter.to(partner).start()
    if pairs > 1:
        grad_gather.forward(1)
        stat_gather.forward(1)

        @pl.loop(1, pairs)
        def _(d):
            @pl.when(d + 1 < pairs)
            def _():
                grad_gather.forward(d + 1)
                stat_gather.forward(d + 1)

            grad_gather.wait_other(d)
            stat_gather.wait_other(d)
            pair = forward_pair_of(d)
            backward_pair(pair)
            for one in range(2):
                query_scatter.to(2 * pair + one).start()

        @pl.loop(1, pairs)
        def _(d):
            att_gather.forward(d)

        att_gather.arrived(partner).wait_recv()

        @pl.loop(1, pairs)
        def _(d):
            att_gather.wait_other(d)
    else:
        att_gather.arrived(partner).wait_recv()

    fg_ref[...] = fg[...]
    att_ref[...] = atall[...]
    query_scatter.wait_all()
    for g in range(groups):
        merged_rows = jnp.sum(dqrecv[:, g].astype(F32), axis=0).T
        for h in range(HEADS_PER_GROUP):
            at = (g * HEADS_PER_GROUP + h) * HEAD_SIZE
            dq_ref[:, at : at + HEAD_SIZE] = merged_rows[h * rows : (h + 1) * rows]

    @pl.loop(1, head)
    def _(d):
        og_copy(me_head, head_peer(d)).wait_send()

    for gather in (query_gather, grad_gather, stat_gather, att_gather):
        gather.drain()
    for scatter in (grad_scatter, out_scatter, stat_scatter, query_scatter):
        scatter.drain()


def body(tok, head, queries, keys, values, out_grad, out_weight, frame_end):
    rows, width = queries.shape
    key_count, key_width = keys.shape
    groups = key_width // HEAD_SIZE
    depth = out_grad.shape[1]
    lanes = HEADS_PER_GROUP * rows
    ends = jnp.broadcast_to(frame_end.reshape(tok, 1, rows), (tok, HEADS_PER_GROUP, rows))
    ends = ends.reshape(tok // 2, 1, 2 * lanes)
    vmem = pl.BlockSpec(memory_space=pltpu.VMEM)
    hbm = pl.BlockSpec(memory_space=pl.ANY)
    dma = pltpu.SemaphoreType.DMA
    query_grad, key_gradient, value_gradient, attended, full_grad = pl.pallas_call(
        functools.partial(kernel, tok, head),
        out_shape=(
            jax.ShapeDtypeStruct((rows, width), F32),
            jax.ShapeDtypeStruct((key_count, key_width), F32),
            jax.ShapeDtypeStruct((key_count, key_width), F32),
            jax.ShapeDtypeStruct((tok, rows, width), BF16),
            jax.ShapeDtypeStruct((head,) + out_grad.shape, BF16),
        ),
        in_specs=[vmem, hbm, hbm, vmem, hbm, vmem],
        out_specs=(vmem,) * 5,
        scratch_shapes=[
            pltpu.VMEM(keys.shape, BF16),
            pltpu.VMEM(values.shape, BF16),
            pltpu.VMEM(out_weight.shape, BF16),
            pltpu.VMEM((groups, HEAD_SIZE, key_count), BF16),
            pltpu.VMEM((groups, HEAD_SIZE, key_count), BF16),
            pltpu.VMEM((head,) + out_grad.shape, BF16),
            pltpu.VMEM((tok, rows, width), BF16),
            pltpu.VMEM((tok, rows, width), BF16),
            pltpu.VMEM((tok, rows, width), BF16),
            pltpu.VMEM((tok, rows, width), BF16),
            pltpu.VMEM((tok // 2, groups, key_count, 2 * lanes), BF16),
            pltpu.VMEM((tok // 2, groups, 1, 2 * lanes), F32),
            pltpu.VMEM((tok, groups, HEAD_SIZE, lanes), BF16),
            pltpu.VMEM((tok, groups, HEAD_SIZE, lanes), BF16),
            pltpu.VMEM((tok, groups, 8, lanes), F32),
            pltpu.VMEM((tok, groups, 8, lanes), F32),
            pltpu.VMEM((tok, groups, 8, lanes), F32),
            pltpu.VMEM((tok, rows, width), BF16),
            pltpu.VMEM((tok, groups, HEAD_SIZE, lanes), BF16),
            pltpu.VMEM((tok, groups, HEAD_SIZE, lanes), BF16),
            dma((3,)),
            dma((head,)),
            dma((head,)),
        ]
        + [dma((tok,)) for _ in range(20)],
        compiler_params=pltpu.CompilerParams(
            collective_id=0, has_side_effects=True, vmem_limit_bytes=56 * 1024 * 1024
        ),
    )(queries, keys, values, out_grad, out_weight, ends)
    row_count = tok * rows
    out_weight_grad = dot(
        attended.reshape(row_count, width), full_grad.reshape(row_count, depth), 0, 0
    )
    return (query_grad, key_gradient, value_gradient, out_weight_grad)


def solution(mesh):
    placed = (
        P("tok", "head"),
        P("tok", "head"),
        P("tok", "head"),
        P("head", "tok"),
        P("head", "tok"),
        P(),
    )
    return jax.shard_map(
        functools.partial(body, mesh.shape["tok"], mesh.shape["head"]),
        mesh=mesh,
        in_specs=placed,
        out_specs=(P("tok", "head"), P("tok", "head"), P("tok", "head"), P("head", "tok")),
        check_vma=False,
    )
```

time: 562 us -> 81.3 us (0.14); the launches traced: 555 us -> 81.1 us
  blocking collectives: 164 us -> 0 us
  loops' own time: 145 us -> 0 us
  matrix products: 96.6 us -> 5.93 us
  waiting for transfers between devices: 81.4 us -> 0 us
  Pallas kernels: 0 us -> 70.5 us
  local copies, waits for them, and re-layouts: 41.5 us -> 4.03 us
  between operations: 14.1 us -> 0.67 us
  other arithmetic: 12.8 us -> 0 us
    all_gather x6 -> x0, blocking collectives: 164 us -> none  [the longest x2 61 us: combined_all(): pieces = jax.tree.map(lambda part: lax.all_gather(part, axis), value)]
    another operation x5 -> x0, loops' own time: 145 us -> none  [the longest x1 62.9 us: body(): output_parts = lax.map(output_part, head_index)]
    dot_general x114 -> x1, matrix products: 96.6 us -> 5.93 us  [dot(): lax.dot_general(left, right, (((left_dim,), (right_dim,)), ((), ())), pre...]
    reduce_scatter x3 -> x0, waiting for transfers between devices: 81.4 us -> none  [the longest x1 54.8 us: body(): lax.psum_scatter(query_terms.astype(jnp.bfloat16), 'tok', scatter_dimensi...]
    pallas_call x0 -> x1, Pallas kernels: none -> 70.5 us  [body(): pl.pallas_call(functools.partial(kernel, tok, head), out_shape=(jax.Shape...]
    dynamic_slice x48 -> x0, local copies, waits for them, and re-layouts: 28.2 us -> none  [the longest x32 18.8 us: body(): row_peaks, row_totals = lax.map(local_totals, head_index)]
    reduce_sum x17 -> x0, other arithmetic: 5.81 us -> none  [the longest x16 4.24 us: local_totals(): jnp.sum(jnp.where(visible, jnp.exp(masked - row_peak[:, None]), 0.0), axi...]
  transfers between devices with their start and end apart: 3 -> 0, of which waited for: 2 -> 0; matrix products, arithmetic and copies ran while one was open for 9% -> 0% of each run, Pallas kernels for 0% -> 0%
where the time goes in v1:
time: 81.3 us; the launch traced here: 81.1 us
  Pallas kernels  70.5 us (87%)
  matrix products  5.93 us (7%)
  local copies, waits for them, and re-layouts  4.03 us (5%)
    pallas_call x1, Pallas kernels, body(): pl.pallas_call(functools.partial(kernel, tok, head), out_shape=(jax.Shape...  70.5 us
    dot_general x1, matrix products, dot(): lax.dot_general(left, right, (((left_dim,), (right_dim,)), ((), ())), pre...  5.93 us
    unnamed x9, local copies, waits for them, and re-layouts  2.61 us

profile of v1, /device:TPU:0, one launch (start us, length us, event | category | flops | bytes accessed | tf_op | source)
XLA Modules:
  0.0 81.1 jit_solution(195606351788407730)
XLA Ops:
  0.6 0.7 broadcast_in_dim.7
  1.4 0.7 reshape.19.fe_ref
  2.1 70.5 %shard_map.93 = (f32[16,2048]{1,0:T(8,128)}, f32[1024,256]{1,0:T(8,128)}, f32[1024,256]{1,0:T(8,128)}, bf16[8,16,2048]{2,1,0:T(8,128)(2,1)}, bf16[4,32,1024]{2,1,0:T(8,128)(2,1)}) custom-call(bf16[16,2048]{1,0:T(8,128)(2,1)} %q_ref.1, bf16[1024,256]{1,0:T(8,128)(2,1)} %k_hbm.1, bf16[1024,256]{1,0:T(8,128)(2,1)} %v_hbm.1, bf16[32,1024]{1,0:T(8,128)(2,1)} %og_ref.1, ...), custom_call_target="tpu_custom_call" | custom-call | tf_op jit(solution)/shard_map/pallas_call | solution.py:371
  72.5 0.0 copy-start.2
  72.5 0.0 copy-start.1
  72.5 0.0 copy-start
  72.6 5.9 %fusion = f32[2048,1024]{1,0:T(8,128)} fusion(bf16[128,2048]{1,0:T(8,128)(2,1)} %bitcast.4, bf16[128,1024]{1,0:T(8,128)(2,1)} %bitcast.5), kind=kOutput, calls=%fused_computation | convolution fusion | flops 536870912 | bytes 9175040 | tf_op jit(solution)/shard_map/dot_general | solution.py:27
  78.5 0.0 copy-done.2
  78.5 0.7 copy.13
  79.1 0.0 copy-done.1
  79.2 1.0 %copy.14 = f32[1024,256]{1,0:T(8,128)} copy(f32[1024,256]{1,0:T(8,128)S(1)} %copy-done.1) | data formatting | bytes 2097152
  80.1 0.0 copy-done
  80.1 1.0 %copy.15 = f32[1024,256]{1,0:T(8,128)} copy(f32[1024,256]{1,0:T(8,128)S(1)} %copy-done) | data formatting | bytes 2097152
  (1 shorter events, 0.0 us)
Async XLA Ops:
  72.5 6.0 %copy-start.2 = (f32[16,2048]{1,0:T(8,128)S(1)}, f32[16,2048]{1,0:T(8,128)}, u32[]{:S(2)}) copy-start(f32[16,2048]{1,0:T(8,128)} %get-tuple-element.18) | copy-start | bytes 393220
  72.5 6.6 %copy-start.1 = (f32[1024,256]{1,0:T(8,128)S(1)}, f32[1024,256]{1,0:T(8,128)}, u32[]{:S(2)}) copy-start(f32[1024,256]{1,0:T(8,128)} %get-tuple-element.19) | copy-start | bytes 3145732
  72.5 7.6 %copy-start = (f32[1024,256]{1,0:T(8,128)S(1)}, f32[1024,256]{1,0:T(8,128)}, u32[]{:S(2)}) copy-start(f32[1024,256]{1,0:T(8,128)} %get-tuple-element.20) | copy-start | bytes 3145732

commit v2 on v1

--- a/solution.py
+++ b/solution.py
@@ -43,10 +43,10 @@
 def kernel(
     tok, head, q_ref, k_hbm, v_hbm, og_ref, ow_hbm, fe_ref,
     dq_ref, dk_ref, dv_ref, att_ref, fg_ref,
-    k_ref, v_ref, ow_ref, kt_ref, vt_ref, fg, qall, gsend, grecv, hgall, pbuf, mbuf,
-    osend, orecv, ssend, srecv, tall, atall, dqsend, dqrecv,
-    load_sem, og_s, og_r, q_s, q_f, q_r, g_s, g_r, h_s, h_f, h_r, o_s, o_r, s_s, s_r,
-    t_s, t_f, t_r, a_s, a_f, a_r, dq_s, dq_r,
+    k_ref, v_ref, ow_ref, kt_ref, vt_ref, fg, qall, gsend, gx, gsum, grecv, hgall, pbuf, mbuf,
+    osend, ox, osum, orecv, ssend, sx, ssum, srecv, tall, atall, dqsend, dqx, dqsum, dqrecv,
+    load_sem, og_s, og_r, q_s, q_f, q_r, h_s, h_f, h_r, a_s, a_f, a_r, t_s, t_r,
+    g_xs, g_xr, g_s, g_r, o_xs, o_xr, o_s, o_r, s_xs, s_xr, s_s, s_r, dq_xs, dq_xr, dq_s, dq_r,
 ):
     me = lax.axis_index("tok")
     me_head = lax.axis_index("head")
@@ -140,37 +140,81 @@
                 self.relay(block).wait_send()
 
     class Scatter:
-        def __init__(self, source, landing, s, r):
-            self.source, self.landing, self.s, self.r = source, landing, s, r
-
-        def to(self, peer):
+        def __init__(self, source, across, summed, landing, xs, xr, s, r):
+            self.source, self.across, self.summed, self.landing = source, across, summed, landing
+            self.xs, self.xr, self.s, self.r = xs, xr, s, r
+
+        def to_partner(self, pair):
             return send(
-                self.source.at[peer], self.landing.at[me], self.s.at[peer], self.r.at[me],
-                {"tok": peer},
+                self.source.at[2 * pair + 1 - side], self.across.at[pair],
+                self.xs.at[pair], self.xr.at[pair], {"tok": partner},
             )
 
+        def along(self, pair, slot):
+            return send(
+                self.summed.at[pair], self.landing.at[slot], self.s.at[pair], self.r.at[slot],
+                {"tok": 2 * pair + side},
+            )
+
         def wait_all(self):
-            @pl.loop(1, tok)
+            @pl.loop(1, pairs)
             def _(d):
-                peer = tok_peer(d)
-                send(
-                    self.source.at[peer], self.landing.at[peer], self.s.at[peer],
-                    self.r.at[peer], {"tok": peer},
-                ).wait_recv()
+                pair = pair_at(d)
+                self.along(pair, pair).wait_recv()
 
         def drain(self):
-            @pl.loop(1, tok)
+            @pl.loop(0, pairs)
             def _(d):
-                self.to(tok_peer(d)).wait_send()
+                self.to_partner(d).wait_send()
+
+            @pl.loop(1, pairs)
+            def _(d):
+                self.along(pair_at(d), my_pair).wait_send()
+
+    def pair_at(d):
+        return lax.rem(my_pair + d, pairs)
+
+    def stat_copy(owner, peer):
+        return send(tall.at[owner], tall.at[owner], t_s.at[peer], t_r.at[owner], {"tok": peer})
 
     query_gather = Gather(qall, q_s, q_f, q_r)
     grad_gather = Gather(hgall, h_s, h_f, h_r)
-    stat_gather = Gather(tall, t_s, t_f, t_r)
     att_gather = Gather(atall, a_s, a_f, a_r)
-    grad_scatter = Scatter(gsend, grecv, g_s, g_r)
-    out_scatter = Scatter(osend, orecv, o_s, o_r)
-    stat_scatter = Scatter(ssend, srecv, s_s, s_r)
-    query_scatter = Scatter(dqsend, dqrecv, dq_s, dq_r)
+    grad_scatter = Scatter(gsend, gx, gsum, grecv, g_xs, g_xr, g_s, g_r)
+    out_scatter = Scatter(osend, ox, osum, orecv, o_xs, o_xr, o_s, o_r)
+    stat_scatter = Scatter(ssend, sx, ssum, srecv, s_xs, s_xr, s_s, s_r)
+    query_scatter = Scatter(dqsend, dqx, dqsum, dqrecv, dq_xs, dq_xr, dq_s, dq_r)
+
+    def sum_on(scatter, pair, own):
+        scatter.to_partner(pair).wait_recv()
+        mine = scatter.source[2 * pair + side].astype(F32)
+        both = (mine + scatter.across[pair].astype(F32)).astype(BF16)
+        if own:
+            scatter.landing[pair] = both
+        else:
+            scatter.summed[pair] = both
+            scatter.along(pair, my_pair).start()
+
+    def merge_on(pair, own):
+        stat_scatter.to_partner(pair).wait_recv()
+        out_scatter.to_partner(pair).wait_recv()
+        for g in range(groups):
+            first, second = ssend[2 * pair + side, g], sx[pair, g]
+            peak = jnp.maximum(first[0:1], second[0:1])
+            w_first, w_second = jnp.exp2(first[0:1] - peak), jnp.exp2(second[0:1] - peak)
+            total = first[1:2] * w_first + second[1:2] * w_second
+            both = osend[2 * pair + side, g].astype(F32) * w_first
+            both = (both + ox[pair, g].astype(F32) * w_second).astype(BF16)
+            stat = jnp.where(row8 == 0, peak, total)
+            if own:
+                orecv[pair, g] = both
+                srecv[pair, g] = stat
+            else:
+                osum[pair, g] = both
+                ssum[pair, g] = stat
+        if not own:
+            stat_scatter.along(pair, my_pair).start()
+            out_scatter.along(pair, my_pair).start()
 
     query_gather.start()
 
@@ -197,11 +241,9 @@
         part = dot(full, ow_ref[pl.ds(start, tile), :], 1, 1).astype(BF16)
         gsend[:, :, pl.ds(start, tile)] = part.reshape(tok, rows, tile)
 
-    grecv[me] = gsend[me]
-
-    @pl.loop(1, tok)
-    def _(d):
-        grad_scatter.to(tok_peer(d)).start()
+    @pl.loop(0, pairs)
+    def _(d):
+        grad_scatter.to_partner(pair_at(d)).start()
 
     def stacked(buf, pair, g):
         pieces = []
@@ -212,11 +254,17 @@
                 pieces.append(block[:, at : at + HEAD_SIZE])
         return jnp.concatenate(pieces, axis=0)
 
-    token = lax.broadcasted_iota(jnp.int32, (key_count, 2 * lanes), 0)
+    row_count = tok * rows
+    token = lax.broadcasted_iota(jnp.int32, (key_count, 2 * lanes), 0).astype(F32)
+    ends = jnp.broadcast_to(fe_ref[...].astype(F32), (8, row_count)).astype(BF16)
+    lane = lax.broadcasted_iota(jnp.int32, (row_count, 2 * lanes), 1)
+    lane_row = (lane // lanes) * rows + lane % rows
+    row_index = lax.broadcasted_iota(jnp.int32, (row_count, 2 * lanes), 0)
     row8 = lax.broadcasted_iota(jnp.int32, (8, lanes), 0)
 
     def forward_pair(pair):
-        limit = fe_ref[pair] * FRAME - me * key_count
+        chosen = (row_index == lane_row + pair * (2 * rows)).astype(F32).astype(BF16)
+        limit = dot(ends, chosen)[0:1] * FRAME - (me * key_count).astype(F32)
         for g in range(groups):
             cols = slice(g * HEAD_SIZE, (g + 1) * HEAD_SIZE)
             scores = dot(k_ref[:, cols], stacked(qall, pair, g), 1, 1) * (SCALE * LOG2E)
@@ -233,15 +281,29 @@
                 osend[2 * pair + one, g] = out[:, part]
                 ssend[2 * pair + one, g] = jnp.where(row8 == 0, peak[:, part], total[:, part])
 
-    forward_pair_of = lambda d: lax.rem(my_pair + d, pairs)
+    def send_out(pair):
+        stat_scatter.to_partner(pair).start()
+        out_scatter.to_partner(pair).start()
+
+    def finish_grad():
+        grad_scatter.wait_all()
+        hgall[me] = jnp.sum(grecv[...].astype(F32), axis=0).astype(BF16)
+        grad_gather.start()
+
+    if pairs > 1:
+        query_gather.forward(1)
     query_gather.arrived(partner).wait_recv()
     forward_pair(my_pair)
-    orecv[me] = osend[me]
-    srecv[me] = ssend[me]
-    stat_scatter.to(partner).start()
-    out_scatter.to(partner).start()
+    send_out(my_pair)
+    sum_on(grad_scatter, my_pair, True)
     if pairs > 1:
-        query_gather.forward(1)
+
+        @pl.loop(1, pairs)
+        def _(d):
+            sum_on(grad_scatter, pair_at(d), False)
+
+    merge_on(my_pair, True)
+    if pairs > 1:
 
         @pl.loop(1, pairs)
         def _(d):
@@ -250,26 +312,33 @@
                 query_gather.forward(d + 1)
 
             query_gather.wait_other(d)
-            pair = forward_pair_of(d)
+
+            @pl.when(d == pairs - 1)
+            def _():
+                finish_grad()
+
+            pair = pair_at(d)
             forward_pair(pair)
-            for one in range(2):
-                stat_scatter.to(2 * pair + one).start()
-                out_scatter.to(2 * pair + one).start()
-
-    grad_scatter.wait_all()
-    hgall[me] = jnp.sum(grecv[...].astype(F32), axis=0).astype(BF16)
-    grad_gather.start()
+            send_out(pair)
+
+            @pl.when(d > 1)
+            def _():
+                merge_on(pair_at(d - 1), False)
+
+        merge_on(pair_at(pairs - 1), False)
+    else:
+        finish_grad()
 
     stat_scatter.wait_all()
     out_scatter.wait_all()
     for g in range(groups):
-        peaks = [srecv[j, g][0:1] for j in range(tok)]
-        totals = [srecv[j, g][1:2] for j in range(tok)]
+        peaks = [srecv[j, g][0:1] for j in range(pairs)]
+        totals = [srecv[j, g][1:2] for j in range(pairs)]
         peak = functools.reduce(jnp.maximum, peaks)
         weights = [jnp.exp2(one - peak) for one in peaks]
         inverse = 1.0 / functools.reduce(jnp.add, [a * b for a, b in zip(weights, totals)])
         merged = jnp.zeros((HEAD_SIZE, lanes), F32)
-        for j in range(tok):
+        for j in range(pairs):
             merged += orecv[j, g].astype(F32) * weights[j]
         merged = (merged * inverse).astype(BF16).astype(F32)
         merged_rows = merged.T
@@ -282,7 +351,11 @@
         grad_t = jnp.concatenate(grad_rows, axis=0).T
         delta = jnp.sum(grad_t * merged, axis=0, keepdims=True)
         tall[me, g] = jnp.where(row8 == 0, peak, jnp.where(row8 == 1, inverse, delta))
-    stat_gather.start()
+
+    @pl.loop(1, tok)
+    def _(d):
+        stat_copy(me, tok_peer(d)).start()
+
     att_gather.start()
 
     dk_ref[...] = jnp.zeros_like(dk_ref)
@@ -303,41 +376,43 @@
             for one in range(2):
                 dqsend[2 * pair + one, g] = query_part[:, one * lanes : (one + 1) * lanes]
 
-    grad_gather.arrived(partner).wait_recv()
-    stat_gather.arrived(partner).wait_recv()
-    backward_pair(my_pair)
-    dqrecv[me] = dqsend[me]
-    query_scatter.to(partner).start()
+    def wait_stat(peer):
+        stat_copy(peer, peer).wait_recv()
+
     if pairs > 1:
         grad_gather.forward(1)
-        stat_gather.forward(1)
+    grad_gather.arrived(partner).wait_recv()
+    wait_stat(partner)
+    backward_pair(my_pair)
+    query_scatter.to_partner(my_pair).start()
+    if pairs > 1:
 
         @pl.loop(1, pairs)
         def _(d):
             @pl.when(d + 1 < pairs)
             def _():
                 grad_gather.forward(d + 1)
-                stat_gather.forward(d + 1)
 
             grad_gather.wait_other(d)
-            stat_gather.wait_other(d)
-            pair = forward_pair_of(d)
+            pair = pair_at(d)
+            wait_stat(2 * pair)
+            wait_stat(2 * pair + 1)
             backward_pair(pair)
-            for one in range(2):
-                query_scatter.to(2 * pair + one).start()
-
-        @pl.loop(1, pairs)
-        def _(d):
+            query_scatter.to_partner(pair).start()
             att_gather.forward(d)
 
-        att_gather.arrived(partner).wait_recv()
+            @pl.when(d > 1)
+            def _():
+                sum_on(query_scatter, pair_at(d - 1), False)
+
+        sum_on(query_scatter, pair_at(pairs - 1), False)
 
         @pl.loop(1, pairs)
         def _(d):
             att_gather.wait_other(d)
-    else:
-        att_gather.arrived(partner).wait_recv()
-
+
+    sum_on(query_scatter, my_pair, True)
+    att_gather.arrived(partner).wait_recv()
     fg_ref[...] = fg[...]
     att_ref[...] = atall[...]
     query_scatter.wait_all()
@@ -351,10 +426,21 @@
     def _(d):
         og_copy(me_head, head_peer(d)).wait_send()
 
-    for gather in (query_gather, grad_gather, stat_gather, att_gather):
+    @pl.loop(1, tok)
+    def _(d):
+        stat_copy(me, tok_peer(d)).wait_send()
+
+    for gather in (query_gather, grad_gather, att_gather):
         gather.drain()
     for scatter in (grad_scatter, out_scatter, stat_scatter, query_scatter):
         scatter.drain()
+
+
+def finish(dq_in, dk_in, dv_in, att_ref, fg_ref, dq_ref, dk_ref, dv_ref, weight_ref):
+    dq_ref[...] = dq_in[...]
+    dk_ref[...] = dk_in[...]
+    dv_ref[...] = dv_in[...]
+    weight_ref[...] = dot(att_ref[...], fg_ref[...], 0, 0)
 
 
 def body(tok, head, queries, keys, values, out_grad, out_weight, frame_end):
@@ -363,8 +449,13 @@
     groups = key_width // HEAD_SIZE
     depth = out_grad.shape[1]
     lanes = HEADS_PER_GROUP * rows
-    ends = jnp.broadcast_to(frame_end.reshape(tok, 1, rows), (tok, HEADS_PER_GROUP, rows))
-    ends = ends.reshape(tok // 2, 1, 2 * lanes)
+    row_count = tok * rows
+    block = pltpu.VMEM((tok, rows, width), BF16)
+    half = pltpu.VMEM((tok // 2, rows, width), BF16)
+    part = pltpu.VMEM((tok, groups, HEAD_SIZE, lanes), BF16)
+    half_part = pltpu.VMEM((tok // 2, groups, HEAD_SIZE, lanes), BF16)
+    stat = pltpu.VMEM((tok, groups, 8, lanes), F32)
+    half_stat = pltpu.VMEM((tok // 2, groups, 8, lanes), F32)
     vmem = pl.BlockSpec(memory_space=pltpu.VMEM)
     hbm = pl.BlockSpec(memory_space=pl.ANY)
     dma = pltpu.SemaphoreType.DMA
@@ -386,32 +477,68 @@
             pltpu.VMEM((groups, HEAD_SIZE, key_count), BF16),
             pltpu.VMEM((groups, HEAD_SIZE, key_count), BF16),
             pltpu.VMEM((head,) + out_grad.shape, BF16),
-            pltpu.VMEM((tok, rows, width), BF16),
-            pltpu.VMEM((tok, rows, width), BF16),
-            pltpu.VMEM((tok, rows, width), BF16),
-            pltpu.VMEM((tok, rows, width), BF16),
+            block,
+            block,
+            half,
+            half,
+            half,
+            block,
             pltpu.VMEM((tok // 2, groups, key_count, 2 * lanes), BF16),
             pltpu.VMEM((tok // 2, groups, 1, 2 * lanes), F32),
-            pltpu.VMEM((tok, groups, HEAD_SIZE, lanes), BF16),
-            pltpu.VMEM((tok, groups, HEAD_SIZE, lanes), BF16),
-            pltpu.VMEM((tok, groups, 8, lanes), F32),
-            pltpu.VMEM((tok, groups, 8, lanes), F32),
-            pltpu.VMEM((tok, groups, 8, lanes), F32),
-            pltpu.VMEM((tok, rows, width), BF16),
-            pltpu.VMEM((tok, groups, HEAD_SIZE, lanes), BF16),
-            pltpu.VMEM((tok, groups, HEAD_SIZE, lanes), BF16),
+            part,
+            half_part,
+            half_part,
+            half_part,
+            stat,
+            half_stat,
+            half_stat,
+            half_stat,
+            stat,
+            block,
+            part,
+            half_part,
+            half_part,
+            half_part,
             dma((3,)),
             dma((head,)),
             dma((head,)),
         ]
-        + [dma((tok,)) for _ in range(20)],
+        + [dma((tok,)) for _ in range(11)]
+        + [dma((tok // 2,)) for _ in range(16)],
         compiler_params=pltpu.CompilerParams(
             collective_id=0, has_side_effects=True, vmem_limit_bytes=56 * 1024 * 1024
         ),
-    )(queries, keys, values, out_grad, out_weight, ends)
-    row_count = tok * rows
-    out_weight_grad = dot(
-        attended.reshape(row_count, width), full_grad.reshape(row_count, depth), 0, 0
+    )(queries, keys, values, out_grad, out_weight, frame_end.reshape(1, row_count))
+    tile = min(256, width)
+    steps = width // tile
+    by_rows = pl.BlockSpec((key_count // steps, key_width), lambda i: (i, 0))
+    by_columns = pl.BlockSpec((rows, tile), lambda i: (0, i))
+    query_grad, key_gradient, value_gradient, out_weight_grad = pl.pallas_call(
+        finish,
+        grid=(steps,),
+        out_shape=(
+            jax.ShapeDtypeStruct((rows, width), F32),
+            jax.ShapeDtypeStruct((key_count, key_width), F32),
+            jax.ShapeDtypeStruct((key_count, key_width), F32),
+            jax.ShapeDtypeStruct((width, depth), F32),
+        ),
+        in_specs=[
+            by_columns,
+            by_rows,
+            by_rows,
+            pl.BlockSpec((row_count, tile), lambda i: (0, i)),
+            pl.BlockSpec((row_count, depth), lambda i: (0, 0)),
+        ],
+        out_specs=(
+            by_columns, by_rows, by_rows, pl.BlockSpec((tile, depth), lambda i: (i, 0))
+        ),
+        compiler_params=pltpu.CompilerParams(vmem_limit_bytes=32 * 1024 * 1024),
+    )(
+        query_grad,
+        key_gradient,
+        value_gradient,
+        attended.reshape(row_count, width),
+        full_grad.reshape(row_count, depth),
     )
     return (query_grad, key_gradient, value_gradient, out_weight_grad)
 

time: 81.3 us -> 80.2 us (0.986)
  matrix products: 5.93 us -> 0 us
  Pallas kernels: 70.5 us -> 73.8 us
  local copies, waits for them, and re-layouts: 4.03 us -> 5.34 us
    dot_general x1 -> x0, matrix products: 5.93 us -> none  [dot(): lax.dot_general(left, right, (((left_dim,), (right_dim,)), ((), ())), pre...]
    pallas_call x0 -> x1, Pallas kernels: none -> 5.69 us  [body(): pl.pallas_call(finish, grid=(steps,), out_shape=(jax.ShapeDtypeStruct((ro...]
    unnamed x9 -> x10, local copies, waits for them, and re-layouts: 2.61 us -> 5.34 us
    pallas_call x1, Pallas kernels: 70.5 us -> 68.1 us  [body(): pl.pallas_call(functools.partial(kernel, tok, head), out_shape=(jax.Shape...]
where the time goes in v2:
time: 80.2 us; the launch traced here: 79.8 us
  Pallas kernels  73.8 us (92%)
  local copies, waits for them, and re-layouts  5.34 us (7%)
    pallas_call x1, Pallas kernels, body(): pl.pallas_call(functools.partial(kernel, tok, head), out_shape=(jax.Shape...  68.1 us
    pallas_call x1, Pallas kernels, body(): pl.pallas_call(finish, grid=(steps,), out_shape=(jax.ShapeDtypeStruct((ro...  5.69 us
    unnamed x10, local copies, waits for them, and re-layouts  5.34 us

profile of v2, /device:TPU:0, one launch (start us, length us, event | category | flops | bytes accessed | tf_op | source)
XLA Modules:
  0.0 79.8 jit_solution(13336644389341967058)
XLA Ops:
  0.6 68.1 %shard_map.93 = (f32[16,2048]{1,0:T(8,128)}, f32[1024,256]{1,0:T(8,128)}, f32[1024,256]{1,0:T(8,128)}, bf16[8,16,2048]{2,1,0:T(8,128)(2,1)}, bf16[4,32,1024]{2,1,0:T(8,128)(2,1)}) custom-call(bf16[16,2048]{1,0:T(8,128)(2,1)} %q_ref.1, bf16[1024,256]{1,0:T(8,128)(2,1)} %k_hbm.1, bf16[1024,256]{1,0:T(8,128)(2,1)} %v_hbm.1, bf16[32,1024]{1,0:T(8,128)(2,1)} %og_ref.1, ...), custom_call_target="tpu_custom_call" | custom-call | tf_op jit(solution)/shard_map/pallas_call | solution.py:462
  68.8 0.0 copy-start
  68.8 1.2 %copy-done = f32[1024,256]{1,0:T(8,128)S(1)} copy-done((f32[1024,256]{1,0:T(8,128)S(1)}, f32[1024,256]{1,0:T(8,128)}, u32[]{:S(2)}) %copy-start) | copy-done | bytes 1048600
  70.0 0.0 copy-start.1
  70.0 1.2 %copy-done.1 = f32[1024,256]{1,0:T(8,128)S(1)} copy-done((f32[1024,256]{1,0:T(8,128)S(1)}, f32[1024,256]{1,0:T(8,128)}, u32[]{:S(2)}) %copy-start.1) | copy-done | bytes 1048600
  71.2 0.0 copy-start.2
  71.2 1.0 %copy-done.2 = bf16[8,16,2048]{2,1,0:T(8,128)(2,1)S(1)} copy-done((bf16[8,16,2048]{2,1,0:T(8,128)(2,1)S(1)}, bf16[8,16,2048]{2,1,0:T(8,128)(2,1)}, u32[]{:S(2)}) %copy-start.2) | copy-done | bytes 524312
  72.3 0.0 copy-start.3
  72.3 0.9 %copy-done.3 = bf16[4,32,1024]{2,1,0:T(8,128)(2,1)S(1)} copy-done((bf16[4,32,1024]{2,1,0:T(8,128)(2,1)S(1)}, bf16[4,32,1024]{2,1,0:T(8,128)(2,1)}, u32[]{:S(2)}) %copy-start.3) | copy-done | bytes 262168
  73.2 0.0 copy-start.4
  73.2 0.9 %copy-done.4 = f32[16,2048]{1,0:T(8,128)S(1)} copy-done((f32[16,2048]{1,0:T(8,128)S(1)}, f32[16,2048]{1,0:T(8,128)}, u32[]{:S(2)}) %copy-start.4) | copy-done | bytes 131096
  74.1 5.7 %shard_map.94 = (f32[16,2048]{1,0:T(8,128)}, f32[1024,256]{1,0:T(8,128)}, f32[1024,256]{1,0:T(8,128)}, f32[2048,1024]{1,0:T(8,128)}) custom-call(f32[16,2048]{1,0:T(8,128)S(1)} %copy-done.4, f32[1024,256]{1,0:T(8,128)S(1)} %copy-done, f32[1024,256]{1,0:T(8,128)S(1)} %copy-done.1, bf16[128,2048]{1,0:T(8,128)(2,1)S(1)} %bitcast.3, bf16[128,1024]{1,0:T(8,128)(2,1)S(1)} %bitcast.4), custom_call_target="tpu_custom_call" | custom-call | tf_op jit(solution)/shard_map/pallas_call | solution.py:516
Async XLA Ops:
  68.8 1.2 %copy-start = (f32[1024,256]{1,0:T(8,128)S(1)}, f32[1024,256]{1,0:T(8,128)}, u32[]{:S(2)}) copy-start(f32[1024,256]{1,0:T(8,128)} %get-tuple-element.10.dk_in) | copy-start | bytes 3145732
  70.0 1.2 %copy-start.1 = (f32[1024,256]{1,0:T(8,128)S(1)}, f32[1024,256]{1,0:T(8,128)}, u32[]{:S(2)}) copy-start(f32[1024,256]{1,0:T(8,128)} %get-tuple-element.11.dv_in) | copy-start | bytes 3145732
  71.2 1.0 %copy-start.2 = (bf16[8,16,2048]{2,1,0:T(8,128)(2,1)S(1)}, bf16[8,16,2048]{2,1,0:T(8,128)(2,1)}, u32[]{:S(2)}) copy-start(bf16[8,16,2048]{2,1,0:T(8,128)(2,1)} %get-tuple-element.12) | copy-start | bytes 1572868
  72.3 0.9 %copy-start.3 = (bf16[4,32,1024]{2,1,0:T(8,128)(2,1)S(1)}, bf16[4,32,1024]{2,1,0:T(8,128)(2,1)}, u32[]{:S(2)}) copy-start(bf16[4,32,1024]{2,1,0:T(8,128)(2,1)} %get-tuple-element.13) | copy-start | bytes 786436
  73.2 0.9 %copy-start.4 = (f32[16,2048]{1,0:T(8,128)S(1)}, f32[16,2048]{1,0:T(8,128)}, u32[]{:S(2)}) copy-start(f32[16,2048]{1,0:T(8,128)} %get-tuple-element.9.dq_in) | copy-start | bytes 393220

commit v3 on v2

--- a/solution.py
+++ b/solution.py
@@ -532,7 +532,7 @@
         out_specs=(
             by_columns, by_rows, by_rows, pl.BlockSpec((tile, depth), lambda i: (i, 0))
         ),
-        compiler_params=pltpu.CompilerParams(vmem_limit_bytes=32 * 1024 * 1024),
+        compiler_params=pltpu.CompilerParams(vmem_limit_bytes=60 * 1024 * 1024),
     )(
         query_grad,
         key_gradient,

time: 80.2 us -> 77.5 us (0.966)
  local copies, waits for them, and re-layouts: 5.34 us -> 0 us
  Pallas kernels: 73.8 us -> 76.5 us
    unnamed x10 -> x0, local copies, waits for them, and re-layouts: 5.34 us -> none
    pallas_call x1, Pallas kernels: 5.69 us -> 8.4 us  [body(): pl.pallas_call(finish, grid=(steps,), out_shape=(jax.ShapeDtypeStruct((ro...]
where the time goes in v3:
time: 77.5 us; the launch traced here: 77.2 us
  Pallas kernels  76.5 us (99%)
    pallas_call x1, Pallas kernels, body(): pl.pallas_call(functools.partial(kernel, tok, head), out_shape=(jax.Shape...  68.1 us
    pallas_call x1, Pallas kernels, body(): pl.pallas_call(finish, grid=(steps,), out_shape=(jax.ShapeDtypeStruct((ro...  8.4 us

profile of v3, /device:TPU:0, one launch (start us, length us, event | category | flops | bytes accessed | tf_op | source)
XLA Modules:
  0.0 77.2 jit_solution(12737192513912322837)
XLA Ops:
  0.6 68.1 %shard_map.93 = (f32[16,2048]{1,0:T(8,128)}, f32[1024,256]{1,0:T(8,128)}, f32[1024,256]{1,0:T(8,128)}, bf16[8,16,2048]{2,1,0:T(8,128)(2,1)}, bf16[4,32,1024]{2,1,0:T(8,128)(2,1)}) custom-call(bf16[16,2048]{1,0:T(8,128)(2,1)} %q_ref.1, bf16[1024,256]{1,0:T(8,128)(2,1)} %k_hbm.1, bf16[1024,256]{1,0:T(8,128)(2,1)} %v_hbm.1, bf16[32,1024]{1,0:T(8,128)(2,1)} %og_ref.1, ...), custom_call_target="tpu_custom_call" | custom-call | tf_op jit(solution)/shard_map/pallas_call | solution.py:462
  68.8 8.4 %shard_map.94 = (f32[16,2048]{1,0:T(8,128)}, f32[1024,256]{1,0:T(8,128)}, f32[1024,256]{1,0:T(8,128)}, f32[2048,1024]{1,0:T(8,128)}) custom-call(f32[16,2048]{1,0:T(8,128)} %get-tuple-element.9.dq_in, f32[1024,256]{1,0:T(8,128)} %get-tuple-element.10.dk_in, f32[1024,256]{1,0:T(8,128)} %get-tuple-element.11.dv_in, bf16[128,2048]{1,0:T(8,128)(2,1)} %bitcast.3, ...), custom_call_target="tpu_custom_call" | custom-call | tf_op jit(solution)/shard_map/pallas_call | solution.py:516
